TPU v7x, 128 devices: a whole 4x4x4 slice. The times are simulated.
128 devices in a mesh: gy: 8 (over x, core), gz: 16 (over y, z).
Axes of the slice: x: 4, y: 4, z: 4, core: 2. Of those that a mesh axis runs over, the one named last changes fastest.
Arguments:
- velocity: float32 [3, 768, 12288], P(None, 'gy', 'gz'), may hold values from -250 to 250
- strain: bfloat16 [6, 768, 12288], P(None, 'gy', 'gz'), may hold values from -250 to 250
- cell_height: float32 [768], P('gy'), may hold values from 0.5 to 2
- stencil_reach: int32 [2, 768], P(None, 'gy'), may hold values from 1 to 8, as said below
Outputs:
- coefficient: float32 [768], P('gy')
Inputs may be any that keep to these rules, and one draw needn't show every extreme that they name: `stencil_reach`: in every draw some plane reaches 8 planes on both sides; stencils are cut at the walls by the steps.
All inputs are finite; a program needn't handle non-finite values.
Results may differ from a plain program's by a relative error of at most 0.0003.
Values sent between devices are 32-bit elements; how exact they have to be, the bound alone decides.
No kernel may reach another device: no remote copies, remote signals or barrier semaphores. Data moves between devices by JAX's collectives and lax.ppermute only.
A program may use at most 128 MiB of HBM per device.

v0:
```python
import jax
import jax.numpy as jnp
from jax import lax
from jax.sharding import PartitionSpec as P

NX = 8
HMAX = 8
LEAD_INDEX = (0, 1, 2, 0, 0, 1)
TAIL_INDEX = (0, 1, 2, 1, 2, 2)
TENSOR_WEIGHTS = (1.0, 1.0, 1.0, 2.0, 2.0, 2.0)


def extended(cells, sides, width, closed):
    for axis, dim in sides:
        count = lax.axis_size(axis)
        ends = count if closed else count - 1
        head = lax.slice_in_dim(cells, 0, width, axis=dim)
        tail = lax.slice_in_dim(cells, cells.shape[dim] - width, cells.shape[dim], axis=dim)
        cells = jnp.concatenate(
            [
                lax.ppermute(tail, axis, [(i, (i + 1) % count) for i in range(ends)]),
                cells,
                lax.ppermute(head, axis, [((i + 1) % count, i) for i in range(ends)]),
            ],
            axis=dim,
        )
    return cells


def strain_rate(tensor):
    squares = 2.0 * (tensor[0] * tensor[0] + tensor[1] * tensor[1] + tensor[2] * tensor[2])
    squares = squares + 4.0 * (
        tensor[3] * tensor[3] + tensor[4] * tensor[4] + tensor[5] * tensor[5]
    )
    return jnp.sqrt(squares)


def form_fields(velocity, tensor):
    products = jnp.stack(
        [
            velocity[first_index] * velocity[second_index]
            for first_index, second_index in zip(LEAD_INDEX, TAIL_INDEX)
        ]
    )
    magnitude = strain_rate(tensor)
    return jnp.concatenate([velocity, products, tensor, magnitude[None] * tensor], axis=0)


def streamwise_filter(fields):
    length = fields.shape[-1]
    position = jnp.arange(length, dtype=jnp.int32) % NX
    behind = jnp.where(
        position == 0, jnp.roll(fields, 1 - NX, axis=-1), jnp.roll(fields, 1, axis=-1)
    )
    ahead_cells = jnp.where(
        position == NX - 1, jnp.roll(fields, NX - 1, axis=-1), jnp.roll(fields, -1, axis=-1)
    )
    return 0.25 * behind + 0.5 * fields + 0.25 * ahead_cells


def spanwise_filter(widened):
    return (
        0.25 * widened[..., : -2 * NX] + 0.5 * widened[..., NX:-NX] + 0.25 * widened[..., 2 * NX :]
    )


def band_apply(band_matrix, padded):
    flattened = padded.reshape(padded.shape[0], padded.shape[1], -1)
    result = jnp.einsum("jc,fcm->fjm", band_matrix, flattened, precision=lax.Precision.HIGHEST)
    return result.reshape((padded.shape[0], band_matrix.shape[0]) + padded.shape[2:])


def contraction(filtered, sum_axes):
    velocity_bar = filtered[0:3]
    product_bar = filtered[3:9]
    tensor_bar = filtered[9:15]
    model_bar = filtered[15:21]
    rate_bar = strain_rate(tensor_bar)
    numerator = jnp.zeros(filtered.shape[1:], jnp.float32)
    denominator = jnp.zeros(filtered.shape[1:], jnp.float32)
    for component in range(6):
        leonard = (
            product_bar[component]
            - velocity_bar[LEAD_INDEX[component]] * velocity_bar[TAIL_INDEX[component]]
        )
        model_term = model_bar[component] - 4.0 * rate_bar * tensor_bar[component]
        numerator = numerator + TENSOR_WEIGHTS[component] * leonard * model_term
        denominator = denominator + TENSOR_WEIGHTS[component] * model_term * model_term
    return (jnp.sum(numerator, axis=sum_axes), jnp.sum(denominator, axis=sum_axes))


def local(velocity, strain, cell_height, stencil_reach):
    planes = velocity.shape[1]
    cell_count = velocity.shape[2]
    total_planes = lax.axis_size("gy") * planes
    total_cells = lax.axis_size("gz") * cell_count
    heights = extended(cell_height, (("gy", 0),), HMAX, False)
    offset = lax.axis_index("gy") * planes
    rows_global = offset + jnp.arange(planes, dtype=jnp.int32)
    columns_global = offset - HMAX + jnp.arange(planes + 2 * HMAX, dtype=jnp.int32)
    lowest = jnp.maximum(rows_global - stencil_reach[0], 0)
    highest = jnp.minimum(rows_global + stencil_reach[1], total_planes - 1)
    inside = (columns_global[None, :] >= lowest[:, None]) & (
        columns_global[None, :] <= highest[:, None]
    )
    weights = jnp.where(inside, heights[None, :], 0.0)
    band_matrix = weights / jnp.sum(weights, axis=1, keepdims=True)
    raw_inputs = jnp.concatenate([velocity, strain.astype(jnp.float32)], axis=0)
    fields = form_fields(raw_inputs[0:3], raw_inputs[3:9])
    widened = extended(streamwise_filter(fields), (("gz", 2),), NX, True)
    spanwise = spanwise_filter(widened)
    full_band = lax.all_gather(band_matrix, "gy", axis=0, tiled=True)
    block_count = lax.axis_size("gy")
    grouped = spanwise.reshape(spanwise.shape[0], planes, block_count, cell_count // block_count)
    padded = jnp.pad(
        lax.all_to_all(grouped, "gy", split_axis=2, concat_axis=1, tiled=True),
        ((0, 0), (HMAX, HMAX), (0, 0), (0, 0)),
    )
    sections = [
        band_apply(
            full_band[block_index * planes : (block_index + 1) * planes],
            padded[:, block_index * planes : block_index * planes + planes + 2 * HMAX],
        )
        for block_index in range(block_count)
    ]
    filtered = jnp.concatenate(sections, axis=1)
    numerator, denominator = contraction(filtered, 1)
    numerator = jnp.sum(numerator, axis=1)
    denominator = jnp.sum(denominator, axis=1)
    numerator, denominator = lax.psum((numerator, denominator), ("gy", "gz"))
    whole = numerator / total_cells / (denominator / total_cells + 1e-06)
    return lax.dynamic_slice_in_dim(whole, offset, planes)


def solution(mesh):
    in_specs = (P(None, "gy", "gz"), P(None, "gy", "gz"), P("gy"), P(None, "gy"))
    out_specs = P("gy")
    return jax.shard_map(local, mesh=mesh, in_specs=in_specs, out_specs=out_specs, check_vma=False)
```

profile of v0, /device:TPU:1, one launch (start us, length us, event | category | flops | bytes accessed | tf_op | source)
XLA Modules:
  0.0 296.6 jit_solution(2417976112965533351)
XLA Ops:
  0.0 1.6 copy.30
  1.6 1.2 constant_dynamic-update-slice_fusion
  2.8 0.8 multiply_dynamic-update-slice_fusion.6
  3.6 0.8 multiply_dynamic-update-slice_fusion.5
  4.4 0.8 multiply_dynamic-update-slice_fusion.4
  5.1 0.8 multiply_dynamic-update-slice_fusion.3
  6.0 0.8 multiply_dynamic-update-slice_fusion.2
  6.8 0.8 multiply_dynamic-update-slice_fusion.1
  7.6 0.7 copy.29
  8.3 0.2 convert_element_type.5
  8.4 1.7 convert_dynamic-update-slice_fusion
  10.1 0.3 fusion.16
  10.4 1.6 multiply_dynamic-update-slice_fusion
  12.0 9.7 %fusion.62 = (f32[21,96,767]{1,2,0:T(8,128)S(1)}, f32[21,96,767]{1,2,0:T(8,128)}) fusion(f32[21,96,768]{1,2,0:T(8,128)} %multiply_dynamic-update-slice_fusion), kind=kLoop, calls=%fused_computation.136 | loop fusion | bytes 24740352 | tf_op jit(solution)/shard_map/jit(_roll_static)/slice | solution.py:56
  21.7 10.9 %fusion.65 = (f32[21,96,761]{1,2,0:T(8,128)}, f32[21,96,761]{1,2,0:T(8,128)}) fusion(f32[21,96,768]{1,2,0:T(8,128)} %multiply_dynamic-update-slice_fusion), kind=kLoop, calls=%fused_computation.139 | loop fusion | bytes 24546816 | tf_op jit(solution)/shard_map/jit(_roll_static)/slice | solution.py:56
  32.6 0.9 fusion.64
  33.5 0.9 fusion.63
  34.5 15.5 %fusion.6 = f32[21,96,768]{1,2,0:T(8,128)S(1)} fusion(f32[21,96,7]{1,2,0:T(8,128)S(1)} %get-tuple-element.16, f32[21,96,761]{1,2,0:T(8,128)} %get-tuple-element.18, f32[21,96,767]{1,2,0:T(8,128)} %get-tuple-element.12, f32[21,96,1]{1,2,0:T(1,128)S(1)} %get-tuple-element.14, f32[21,96,761]{1,2,0:T(8,128)} %get-tuple-element.17, ...), kind=kLoop, calls=%fused_computation.9 | loop fusion | flops 17031168 | bytes 37160448 | tf_op jit(solution)/shard_map/add | solution.py:58
  50.0 2.5 collective-permute-start
  52.5 4.7 %collective-permute-start.1 = (f32[21,96,8]{1,2,0:T(8,128)S(1)}, f32[21,96,8]{1,2,0:T(8,128)S(1)}, u32[]{:S(2)}, u32[]{:S(2)}) collective-permute-start(f32[21,96,8]{1,2,0:T(8,128)S(1)} %get-tuple-element.10), channel_id=1, source_target_pairs={{1,0},{2,1},{3,2},{4,3},{5,4},{6,5},{7,6},{8,7},{9,8},{10,9},{11,1... | collective-permute-start | bytes 193544 | tf_op jit(solution)/shard_map/ppermute | solution.py:23
  57.2 2.2 collective-permute-done
  59.4 2.4 fusion.1
  61.8 3.9 %copy.31 = f32[21,96,8,96]{1,3,0,2:T(8,128)} copy(f32[21,96,8,96]{1,3,2,0:T(8,128)S(1)} %bitcast.280) | data formatting | bytes 12386304 | tf_op jit(solution)/shard_map/reshape | solution.py:114
  65.7 6.2 %all-to-all-start = ((f32[21,96,8,96]{1,3,0,2:T(8,128)}), f32[21,96,8,96]{1,3,0,2:T(8,128)}, u32[]{:S(2)}, u32[]{:S(2)}) async-start(f32[21,96,8,96]{1,3,0,2:T(8,128)} %copy.31), calls=%async_computation | async-start | bytes 16515072 | tf_op jit(solution)/shard_map/all_to_all | solution.py:116
  71.9 0.1 fusion.66
  72.0 3.5 %collective-permute-start.2 = (f32[8]{0:T(128)S(1)}, f32[8]{0:T(128)S(1)}, u32[]{:S(2)}, u32[]{:S(2)}) collective-permute-start(f32[8]{0:T(128)S(1)} %get-tuple-element.21), channel_id=1, source_target_pairs={{0,16},{16,32},{32,48},{48,64},{64,80},{80,96},{96,112},{1,17},{17... | collective-permute-start | bytes 104 | tf_op jit(solution)/shard_map/ppermute | solution.py:21
  75.5 1.9 collective-permute-start.3
  77.5 83.5 %collective-permute-done.2 = f32[8]{0:T(128)S(1)} collective-permute-done((f32[8]{0:T(128)S(1)}, f32[8]{0:T(128)S(1)}, u32[]{:S(2)}, u32[]{:S(2)}) %collective-permute-start.2) | collective-permute-done | bytes 64 | tf_op jit(solution)/shard_map/ppermute | solution.py:21
  160.9 2.4 collective-permute-done.3
  163.3 0.1 pad_maximum_fusion.2
  163.4 0.2 select_reduce_fusion
  163.6 0.1 select_divide_fusion
  163.7 11.9 %all_gather.3 = f32[768,112]{1,0:T(8,128)S(1)} all-gather(f32[96,112]{1,0:T(8,128)S(1)} %select_divide_fusion), channel_id=1, replica_groups=mesh['gy'=8,'gz'=16] {'gy'}, dimensions={0}, use_global_device_ids=true | all-gather | bytes 387072 | tf_op jit(solution)/shard_map/all_gather | solution.py:112
  175.6 13.4 %copy.32 = f32[21,8,96,1,96]{2,1,4,0,3:T(8,128)} copy(f32[21,8,96,1,96]{2,4,0,1,3:T(8,128)} %bitcast.3) | data formatting | bytes 12386304 | tf_op jit(solution)/shard_map/all_to_all | solution.py:116
  189.0 9.5 %all_to_all.16 = f32[21,768,1,96]{1,3,0,2:T(8,128)} reshape(f32[21,8,96,1,96]{2,1,4,0,3:T(8,128)} %copy.32) | data formatting | bytes 12386304 | tf_op jit(solution)/shard_map/all_to_all | solution.py:116
  198.5 2.4 convolution_bitcast_fusion
  200.9 2.6 convolution_bitcast_fusion.1
  203.5 2.0 convolution_bitcast_fusion.2
  205.5 2.0 convolution_bitcast_fusion.3
  207.5 2.1 convolution_bitcast_fusion.4
  209.5 2.0 convolution_bitcast_fusion.5
  211.5 2.0 convolution_bitcast_fusion.6
  213.5 1.0 convolution_bitcast_fusion.7
  214.6 8.9 %concatenate.40 = f32[21,768,1,96]{1,3,0,2:T(8,128)} concatenate(f32[21,96,1,96]{1,3,0,2:T(8,128)S(1)} %convolution_bitcast_fusion.7, f32[21,96,1,96]{1,3,0,2:T(8,128)} %convolution_bitcast_fusion.6, f32[21,96,1,96]{1,3,0,2:T(8,128)} %convolution_bitcast_fusion.5, f32[21,96,1,96]{1,3,0,2:T(8,128)} %convolution_bitcast_fusion.4, f32[21,96,1,96]{1,3,0,2:T(8,128)} %convolution_bitcast_fusion.3, ...), dimensions={1} | concatenate | bytes 12386304 | tf_op jit(solution)/shard_map/concatenate | solution.py:126
  223.4 3.3 %fusion.30 = (f32[768]{0:T(1024)S(1)}, f32[768,96]{0,1:T(8,128)S(1)}) fusion(f32[21,768,1,96]{1,3,2,0:T(8,128)} %bitcast.278, f32[21,768,1,96]{1,3,0,2:T(8,128)} %concatenate.40), kind=kLoop, calls=%fused_computation.67 | loop fusion | flops 3906816 | bytes 6491136 | tf_op jit(solution)/shard_map/reduce_sum | solution.py:128
  226.7 2.2 fusion.24
  229.0 67.1 %all-reduce.1 = (f32[768]{0:T(1024)S(1)}, f32[768]{0:T(1024)S(1)}) all-reduce(f32[768]{0:T(1024)S(1)} %fusion.24, f32[768]{0:T(1024)S(1)} %get-tuple-element.7), channel_id=1, replica_groups=mesh['gy'=8,'gz'=16] {'gy','gz'}, use_global_device_ids=true, to_apply=%region_4.5 | all-reduce | flops 1536 | bytes 12288 | tf_op jit(solution)/shard_map/psum | solution.py:130
  296.0 0.6 dynamic_slice.3
  (15 shorter events, 0.1 us)
Async XLA Ops:
  0.0 7.5 %copy-start.1 = (bf16[6,96,768]{2,1,0:T(8,128)(2,1)S(1)}, bf16[6,96,768]{2,1,0:T(8,128)(2,1)}, u32[]{:S(2)}) copy-start(bf16[6,96,768]{2,1,0:T(8,128)(2,1)} %param.5) | copy-start | bytes 2654212
  50.0 9.4 %collective-permute-start = (f32[21,96,8]{1,2,0:T(8,128)S(1)}, f32[21,96,8]{1,2,0:T(8,128)S(1)}, u32[]{:S(2)}, u32[]{:S(2)}) collective-permute-start(f32[21,96,8]{1,2,0:T(8,128)S(1)} %get-tuple-element.9), channel_id=1, source_target_pairs={{0,1},{1,2},{2,3},{3,4},{4,5},{5,6},{6,7},{7,8},{8,9},{9,10},{10,1... | collective-permute-start | bytes 193544 | tf_op jit(solution)/shard_map/ppermute | solution.py:21
  52.5 6.8 %collective-permute-start.1 = (f32[21,96,8]{1,2,0:T(8,128)S(1)}, f32[21,96,8]{1,2,0:T(8,128)S(1)}, u32[]{:S(2)}, u32[]{:S(2)}) collective-permute-start(f32[21,96,8]{1,2,0:T(8,128)S(1)} %get-tuple-element.10), channel_id=1, source_target_pairs={{1,0},{2,1},{3,2},{4,3},{5,4},{6,5},{7,6},{8,7},{9,8},{10,9},{11,1... | collective-permute-start | bytes 193544 | tf_op jit(solution)/shard_map/ppermute | solution.py:23
  65.7 6.2 %copy-start.2 = (f32[96]{0:T(128)S(1)}, f32[96]{0:T(128)}, u32[]{:S(2)}) copy-start(f32[96]{0:T(128)} %param.6) | copy-start | bytes 1156
  65.7 11.7 %copy-start.3 = (s32[2,96]{1,0:T(2,128)S(1)}, s32[2,96]{1,0:T(2,128)}, u32[]{:S(2)}) copy-start(s32[2,96]{1,0:T(2,128)} %param.7) | copy-start | bytes 2308
  65.7 109.9 %all-to-all-start = ((f32[21,96,8,96]{1,3,0,2:T(8,128)}), f32[21,96,8,96]{1,3,0,2:T(8,128)}, u32[]{:S(2)}, u32[]{:S(2)}) async-start(f32[21,96,8,96]{1,3,0,2:T(8,128)} %copy.31), calls=%async_computation | async-start | bytes 16515072 | tf_op jit(solution)/shard_map/all_to_all | solution.py:116
  72.0 89.0 %collective-permute-start.2 = (f32[8]{0:T(128)S(1)}, f32[8]{0:T(128)S(1)}, u32[]{:S(2)}, u32[]{:S(2)}) collective-permute-start(f32[8]{0:T(128)S(1)} %get-tuple-element.21), channel_id=1, source_target_pairs={{0,16},{16,32},{32,48},{48,64},{64,80},{80,96},{96,112},{1,17},{17... | collective-permute-start | bytes 104 | tf_op jit(solution)/shard_map/ppermute | solution.py:21
  75.5 87.8 %collective-permute-start.3 = (f32[8]{0:T(128)S(1)}, f32[8]{0:T(128)S(1)}, u32[]{:S(2)}, u32[]{:S(2)}) collective-permute-start(f32[8]{0:T(128)S(1)} %get-tuple-element.22), channel_id=1, source_target_pairs={{16,0},{32,16},{48,32},{64,48},{80,64},{96,80},{112,96},{17,1},{33... | collective-permute-start | bytes 104 | tf_op jit(solution)/shard_map/ppermute | solution.py:23
  198.5 5.0 %copy-start = (f32[21,768,1,96]{1,3,0,2:T(8,128)S(1)}, f32[21,768,1,96]{1,3,0,2:T(8,128)}, u32[]{:S(2)}) copy-start(f32[21,768,1,96]{1,3,0,2:T(8,128)} %all_to_all.16) | copy-start | bytes 18579460
where the time goes:
time: 297 us
  waiting for transfers between devices  88 us (30%)
  blocking collectives  79 us (27%)
  local copies, waits for them, and re-layouts  62.3 us (21%)
  other arithmetic  32.3 us (11%)
  starting transfers between devices  18.8 us (6%)
  matrix products  16 us (5%)
    ppermute x2, waiting for transfers between devices, extended(): lax.ppermute(tail, axis, [(i, (i + 1) % count) for i in range(ends)])  85.6 us
    psum x1, blocking collectives, local(): numerator, denominator = lax.psum((numerator, denominator), ('gy', 'gz'))  67.1 us
    all_to_all x2, local copies, waits for them, and re-layouts, local(): lax.all_to_all(grouped, 'gy', split_axis=2, concat_axis=1, tiled=True)  22.9 us
    dot_general x8, matrix products, band_apply(): jnp.einsum('jc,fcm->fjm', band_matrix, flattened, precision=lax.Precision...  16 us
    add x1, other arithmetic, streamwise_filter(): return 0.25 * behind + 0.5 * fields + 0.25 * ahead_cells  15.5 us
    all_gather x1, blocking collectives, local(): full_band = lax.all_gather(band_matrix, 'gy', axis=0, tiled=True)  11.9 us
    slice x2, local copies, waits for them, and re-layouts, streamwise_filter(): jnp.roll(fields, NX - 1, axis=-1)  11.9 us
    slice x2, local copies, waits for them, and re-layouts, streamwise_filter(): jnp.roll(fields, -1, axis=-1)  10.6 us
  transfers between devices with their start and end apart: 5, of which 3 were waited for; matrix products, arithmetic and copies ran while one was open for 0% of the time, Pallas kernels for 0%

commit v1 on v0

--- a/solution.py
+++ b/solution.py
@@ -127,7 +127,7 @@
     numerator, denominator = contraction(filtered, 1)
     numerator = jnp.sum(numerator, axis=1)
     denominator = jnp.sum(denominator, axis=1)
-    numerator, denominator = lax.psum((numerator, denominator), ("gy", "gz"))
+    numerator, denominator = lax.psum(lax.psum((numerator, denominator), "gy"), "gz")
     whole = numerator / total_cells / (denominator / total_cells + 1e-06)
     return lax.dynamic_slice_in_dim(whole, offset, planes)
 

time: 297 us -> 286 us (0.963)
  the two profiles are of different devices: /device:TPU:1 before, /device:TPU:0 now
where the time goes in v1:
time: 286 us; the launch traced here: 285 us
  blocking collectives  154 us (54%)
  local copies, waits for them, and re-layouts  62.3 us (22%)
  other arithmetic  32.3 us (11%)
  matrix products  16 us (6%)
  starting transfers between devices  15.3 us (5%)
  waiting for transfers between devices  5.26 us (2%)
    all_gather x1, blocking collectives, local(): full_band = lax.all_gather(band_matrix, 'gy', axis=0, tiled=True)  96.8 us
    psum x1, blocking collectives, local(): lax.psum(lax.psum((numerator, denominator), 'gy'), 'gz')  41.3 us
    all_to_all x2, local copies, waits for them, and re-layouts, local(): lax.all_to_all(grouped, 'gy', split_axis=2, concat_axis=1, tiled=True)  22.9 us
    dot_general x8, matrix products, band_apply(): jnp.einsum('jc,fcm->fjm', band_matrix, flattened, precision=lax.Precision...  16 us
    psum x1, blocking collectives, local(): lax.psum((numerator, denominator), 'gy')  15.6 us
    add x1, other arithmetic, streamwise_filter(): return 0.25 * behind + 0.5 * fields + 0.25 * ahead_cells  15.5 us
    slice x2, local copies, waits for them, and re-layouts, streamwise_filter(): jnp.roll(fields, NX - 1, axis=-1)  11.8 us
    slice x2, local copies, waits for them, and re-layouts, streamwise_filter(): jnp.roll(fields, -1, axis=-1)  10.6 us
  transfers between devices with their start and end apart: 5, of which 2 were waited for; matrix products, arithmetic and copies ran while one was open for 0% of the time, Pallas kernels for 0%

profile of v1, /device:TPU:0, one launch (start us, length us, event | category | flops | bytes accessed | tf_op | source)
XLA Modules:
  0.0 285.1 jit_solution(5808550794841654113)
XLA Ops:
  0.0 1.6 copy.30
  1.6 1.2 constant_dynamic-update-slice_fusion
  2.8 0.8 multiply_dynamic-update-slice_fusion.6
  3.6 0.8 multiply_dynamic-update-slice_fusion.5
  4.4 0.8 multiply_dynamic-update-slice_fusion.4
  5.1 0.8 multiply_dynamic-update-slice_fusion.3
  6.0 0.8 multiply_dynamic-update-slice_fusion.2
  6.8 0.8 multiply_dynamic-update-slice_fusion.1
  7.6 0.7 copy.29
  8.3 0.2 convert_element_type.5
  8.4 1.7 convert_dynamic-update-slice_fusion
  10.1 0.3 fusion.16
  10.4 1.6 multiply_dynamic-update-slice_fusion
  12.0 9.7 %fusion.62 = (f32[21,96,767]{1,2,0:T(8,128)S(1)}, f32[21,96,767]{1,2,0:T(8,128)}) fusion(f32[21,96,768]{1,2,0:T(8,128)} %multiply_dynamic-update-slice_fusion), kind=kLoop, calls=%fused_computation.136 | loop fusion | bytes 24740352 | tf_op jit(solution)/shard_map/jit(_roll_static)/slice | solution.py:56
  21.6 10.9 %fusion.65 = (f32[21,96,761]{1,2,0:T(8,128)}, f32[21,96,761]{1,2,0:T(8,128)}) fusion(f32[21,96,768]{1,2,0:T(8,128)} %multiply_dynamic-update-slice_fusion), kind=kLoop, calls=%fused_computation.139 | loop fusion | bytes 24546816 | tf_op jit(solution)/shard_map/jit(_roll_static)/slice | solution.py:56
  32.5 0.9 fusion.64
  33.5 0.9 fusion.63
  34.4 15.5 %fusion.6 = f32[21,96,768]{1,2,0:T(8,128)S(1)} fusion(f32[21,96,7]{1,2,0:T(8,128)S(1)} %get-tuple-element.18, f32[21,96,761]{1,2,0:T(8,128)} %get-tuple-element.20, f32[21,96,767]{1,2,0:T(8,128)} %get-tuple-element.14, f32[21,96,1]{1,2,0:T(1,128)S(1)} %get-tuple-element.16, f32[21,96,761]{1,2,0:T(8,128)} %get-tuple-element.19, ...), kind=kLoop, calls=%fused_computation.9 | loop fusion | flops 17031168 | bytes 37160448 | tf_op jit(solution)/shard_map/add | solution.py:58
  49.9 2.1 collective-permute-start
  52.0 4.7 %collective-permute-start.1 = (f32[21,96,8]{1,2,0:T(8,128)S(1)}, f32[21,96,8]{1,2,0:T(8,128)S(1)}, u32[]{:S(2)}, u32[]{:S(2)}) collective-permute-start(f32[21,96,8]{1,2,0:T(8,128)S(1)} %get-tuple-element.12), channel_id=1, source_target_pairs={{1,0},{2,1},{3,2},{4,3},{5,4},{6,5},{7,6},{8,7},{9,8},{10,9},{11,1... | collective-permute-start | bytes 193544 | tf_op jit(solution)/shard_map/ppermute | solution.py:23
  56.6 2.4 collective-permute-done
  59.1 2.4 fusion.1
  61.5 3.9 %copy.31 = f32[21,96,8,96]{1,3,0,2:T(8,128)} copy(f32[21,96,8,96]{1,3,2,0:T(8,128)S(1)} %bitcast.280) | data formatting | bytes 12386304 | tf_op jit(solution)/shard_map/reshape | solution.py:114
  65.5 5.1 %all-to-all-start = ((f32[21,96,8,96]{1,3,0,2:T(8,128)}), f32[21,96,8,96]{1,3,0,2:T(8,128)}, u32[]{:S(2)}, u32[]{:S(2)}) async-start(f32[21,96,8,96]{1,3,0,2:T(8,128)} %copy.31), calls=%async_computation | async-start | bytes 16515072 | tf_op jit(solution)/shard_map/all_to_all | solution.py:116
  70.5 0.1 fusion.66
  70.6 2.3 collective-permute-start.2
  72.9 1.3 collective-permute-start.3
  74.2 2.8 collective-permute-done.3
  77.0 0.1 pad_maximum_fusion.2
  77.1 0.2 select_reduce_fusion
  77.3 0.1 select_divide_fusion
  77.4 96.8 %all_gather.3 = f32[768,112]{1,0:T(8,128)S(1)} all-gather(f32[96,112]{1,0:T(8,128)S(1)} %select_divide_fusion), channel_id=1, replica_groups=mesh['gy'=8,'gz'=16] {'gy'}, dimensions={0}, use_global_device_ids=true | all-gather | bytes 387072 | tf_op jit(solution)/shard_map/all_gather | solution.py:112
  174.3 13.4 %copy.32 = f32[21,8,96,1,96]{2,1,4,0,3:T(8,128)} copy(f32[21,8,96,1,96]{2,4,0,1,3:T(8,128)} %bitcast.3) | data formatting | bytes 12386304 | tf_op jit(solution)/shard_map/all_to_all | solution.py:116
  187.7 9.5 %all_to_all.16 = f32[21,768,1,96]{1,3,0,2:T(8,128)} reshape(f32[21,8,96,1,96]{2,1,4,0,3:T(8,128)} %copy.32) | data formatting | bytes 12386304 | tf_op jit(solution)/shard_map/all_to_all | solution.py:116
  197.2 2.4 convolution_bitcast_fusion
  199.6 2.6 convolution_bitcast_fusion.1
  202.2 2.0 convolution_bitcast_fusion.2
  204.2 2.0 convolution_bitcast_fusion.3
  206.1 2.1 convolution_bitcast_fusion.4
  208.2 2.0 convolution_bitcast_fusion.5
  210.2 2.0 convolution_bitcast_fusion.6
  212.2 1.0 convolution_bitcast_fusion.7
  213.2 8.9 %concatenate.40 = f32[21,768,1,96]{1,3,0,2:T(8,128)} concatenate(f32[21,96,1,96]{1,3,0,2:T(8,128)S(1)} %convolution_bitcast_fusion.7, f32[21,96,1,96]{1,3,0,2:T(8,128)} %convolution_bitcast_fusion.6, f32[21,96,1,96]{1,3,0,2:T(8,128)} %convolution_bitcast_fusion.5, f32[21,96,1,96]{1,3,0,2:T(8,128)} %convolution_bitcast_fusion.4, f32[21,96,1,96]{1,3,0,2:T(8,128)} %convolution_bitcast_fusion.3, ...), dimensions={1} | concatenate | bytes 12386304 | tf_op jit(solution)/shard_map/concatenate | solution.py:126
  222.1 3.3 %fusion.30 = (f32[768]{0:T(1024)S(1)}, f32[768,96]{0,1:T(8,128)S(1)}) fusion(f32[21,768,1,96]{1,3,2,0:T(8,128)} %bitcast.278, f32[21,768,1,96]{1,3,0,2:T(8,128)} %concatenate.40), kind=kLoop, calls=%fused_computation.67 | loop fusion | flops 3906816 | bytes 6491136 | tf_op jit(solution)/shard_map/reduce_sum | solution.py:128
  225.4 2.2 fusion.24
  227.6 15.6 %all-reduce.2 = (f32[768]{0:T(1024)S(1)}, f32[768]{0:T(1024)S(1)}) all-reduce(f32[768]{0:T(1024)S(1)} %fusion.24, f32[768]{0:T(1024)S(1)} %get-tuple-element.9), channel_id=1, replica_groups=mesh['gy'=8,'gz'=16] {'gy'}, use_global_device_ids=true, to_apply=%region_5.6 | all-reduce | flops 1536 | bytes 12288 | tf_op jit(solution)/shard_map/psum | solution.py:130
  243.2 41.3 %all-reduce.1 = (f32[768]{0:T(1024)S(1)}, f32[768]{0:T(1024)S(1)}) all-reduce(f32[768]{0:T(1024)S(1)} %get-tuple-element.7, f32[768]{0:T(1024)S(1)} %get-tuple-element.8), channel_id=1, replica_groups=mesh['gy'=8,'gz'=16] {'gz'}, use_global_device_ids=true, to_apply=%region_6.7 | all-reduce | flops 1536 | bytes 12288 | tf_op jit(solution)/shard_map/psum | solution.py:130
  284.6 0.6 dynamic_slice.3
  (16 shorter events, 0.1 us)
Async XLA Ops:
  0.0 7.6 %copy-start.1 = (bf16[6,96,768]{2,1,0:T(8,128)(2,1)S(1)}, bf16[6,96,768]{2,1,0:T(8,128)(2,1)}, u32[]{:S(2)}) copy-start(bf16[6,96,768]{2,1,0:T(8,128)(2,1)} %param.5) | copy-start | bytes 2654212
  49.9 9.2 %collective-permute-start = (f32[21,96,8]{1,2,0:T(8,128)S(1)}, f32[21,96,8]{1,2,0:T(8,128)S(1)}, u32[]{:S(2)}, u32[]{:S(2)}) collective-permute-start(f32[21,96,8]{1,2,0:T(8,128)S(1)} %get-tuple-element.11), channel_id=1, source_target_pairs={{0,1},{1,2},{2,3},{3,4},{4,5},{5,6},{6,7},{7,8},{8,9},{9,10},{10,1... | collective-permute-start | bytes 193544 | tf_op jit(solution)/shard_map/ppermute | solution.py:21
  52.0 7.1 %collective-permute-start.1 = (f32[21,96,8]{1,2,0:T(8,128)S(1)}, f32[21,96,8]{1,2,0:T(8,128)S(1)}, u32[]{:S(2)}, u32[]{:S(2)}) collective-permute-start(f32[21,96,8]{1,2,0:T(8,128)S(1)} %get-tuple-element.12), channel_id=1, source_target_pairs={{1,0},{2,1},{3,2},{4,3},{5,4},{6,5},{7,6},{8,7},{9,8},{10,9},{11,1... | collective-permute-start | bytes 193544 | tf_op jit(solution)/shard_map/ppermute | solution.py:23
  65.5 5.1 %copy-start.2 = (f32[96]{0:T(128)S(1)}, f32[96]{0:T(128)}, u32[]{:S(2)}) copy-start(f32[96]{0:T(128)} %param.6) | copy-start | bytes 1156
  65.5 8.7 %copy-start.3 = (s32[2,96]{1,0:T(2,128)S(1)}, s32[2,96]{1,0:T(2,128)}, u32[]{:S(2)}) copy-start(s32[2,96]{1,0:T(2,128)} %param.7) | copy-start | bytes 2308
  65.5 108.8 %all-to-all-start = ((f32[21,96,8,96]{1,3,0,2:T(8,128)}), f32[21,96,8,96]{1,3,0,2:T(8,128)}, u32[]{:S(2)}, u32[]{:S(2)}) async-start(f32[21,96,8,96]{1,3,0,2:T(8,128)} %copy.31), calls=%async_computation | async-start | bytes 16515072 | tf_op jit(solution)/shard_map/all_to_all | solution.py:116
  70.6 3.6 %collective-permute-start.2 = (f32[8]{0:T(128)S(1)}, f32[8]{0:T(128)S(1)}, u32[]{:S(2)}, u32[]{:S(2)}) collective-permute-start(f32[8]{0:T(128)S(1)} %get-tuple-element.23), channel_id=1, source_target_pairs={{0,16},{16,32},{32,48},{48,64},{64,80},{80,96},{96,112},{1,17},{17... | collective-permute-start | bytes 104 | tf_op jit(solution)/shard_map/ppermute | solution.py:21
  72.9 4.2 %collective-permute-start.3 = (f32[8]{0:T(128)S(1)}, f32[8]{0:T(128)S(1)}, u32[]{:S(2)}, u32[]{:S(2)}) collective-permute-start(f32[8]{0:T(128)S(1)} %get-tuple-element.24), channel_id=1, source_target_pairs={{16,0},{32,16},{48,32},{64,48},{80,64},{96,80},{112,96},{17,1},{33... | collective-permute-start | bytes 104 | tf_op jit(solution)/shard_map/ppermute | solution.py:23
  197.2 5.0 %copy-start = (f32[21,768,1,96]{1,3,0,2:T(8,128)S(1)}, f32[21,768,1,96]{1,3,0,2:T(8,128)}, u32[]{:S(2)}) copy-start(f32[21,768,1,96]{1,3,0,2:T(8,128)} %all_to_all.16) | copy-start | bytes 18579460
